TPU v7x, 128 devices: a whole 4x4x4 slice. The times are simulated.
128 devices in a mesh: inner: 8 (over z_hi, x), outer: 16 (over z_lo, y, core).
Axes of the slice: x: 4, y: 4, z: 4 (z_hi: 2, z_lo: 2; z = z_hi * 2 + z_lo), core: 2. Of those that a mesh axis runs over, the one named last changes fastest.
Arguments:
- image_embed: bfloat16 [16384, 768], P(('inner', 'outer')), may hold values from -80 to 80
- text_embed: bfloat16 [16384, 768], P(('inner', 'outer')), may hold values from -32 to 32
Outputs:
- mean_loss: float32 [], replicated
- image_grad: float32 [16384, 768], P(('inner', 'outer'))
- text_grad: float32 [16384, 768], P(('inner', 'outer'))
All inputs are finite; a program needn't handle non-finite values.
Results may differ from a plain program's by a relative error of at most 0.0023.
Values may be sent and summed in bfloat16 or wider, within the bound.
A program may use at most 192 MiB of HBM per device.

v0:
```python
import functools
import math

import jax
import jax.numpy as jnp
from jax import lax
from jax.experimental import pallas as pl
from jax.experimental.pallas import tpu as pltpu
from jax.sharding import PartitionSpec as P

F32, BF16 = jnp.float32, jnp.bfloat16
MESH = pl.DeviceIdType.MESH
OFFSETS = ((0, 0), (0, 1), (0, 3), (0, 2), (1, 0), (1, 1), (1, 3), (1, 2))
PLACE = (0, 2, 3, 4, 1, 5, 6, 7)
RING = 4
SLOTS = 8
LOG2E = math.log2(math.e)


def add_up(values):
    return functools.reduce(jnp.add, values)


class Group:
    def __init__(self, kind):
        inner, outer = lax.axis_index("inner"), lax.axis_index("outer")
        core, chip = lax.rem(outer, 2), outer // 2
        high, x = inner // RING, lax.rem(inner, RING)
        low, y = chip // RING, lax.rem(chip, RING)
        self.kind, self.y = kind, y
        self.place = y if kind else x
        self.cores, self.lows, self.highs = (core, 1 - core), (low, 1 - low), (high, 1 - high)
        self.places = [self.place] + [lax.rem(self.place + n, RING) for n in range(1, RING)]

    def index(self, plane_step, ring_step, core_step=0):
        if self.kind == 0:
            return self.highs[plane_step] * RING + self.places[ring_step]
        chip = self.lows[plane_step] * RING + self.places[ring_step]
        return chip * 2 + self.cores[core_step]

    def device(self, plane_step, ring_step, core_step=0):
        index = self.index(plane_step, ring_step, core_step)
        if self.kind:
            return {"outer": index}
        chip = self.lows[plane_step] * RING + self.y
        return {"inner": index, "outer": chip * 2 + self.cores[0]}


def kernel(
    image_ref,
    text_ref,
    loss_ref,
    image_out,
    text_out,
    image_rows,
    text_rows,
    scores,
    row_top,
    row_sum,
    col_top,
    col_sum,
    row_stats,
    col_stats,
    row_lse,
    col_lse,
    row_wide,
    col_wide,
    w_own,
    w_other,
    w_got,
    image_part,
    text_part,
    image_send,
    text_send,
    image_got,
    text_got,
    image_loss,
    image_loss_ring,
    text_loss,
    text_loss_ring,
    gather_send,
    gather_recv,
    fwd_send,
    fwd_recv,
    row_ssem,
    row_rsem,
    col_ssem,
    col_rsem,
    loss_ssem,
    loss_rsem,
    w_ssem,
    w_rsem,
    red_ssem,
    red_rsem,
    load_sem,
):
    block, width = image_ref.shape
    half = block // 2
    pair = 2 * block
    scale = width ** (-0.5)
    inner, outer = lax.axis_index("inner"), lax.axis_index("outer")
    groups = (Group(0), Group(1))
    sibling = {"outer": groups[1].index(0, 0, 1)}
    rows = (image_rows, text_rows)

    def remote(src, dst, ssem, rsem, device):
        return pltpu.make_async_remote_copy(
            src_ref=src,
            dst_ref=dst,
            send_sem=ssem,
            recv_sem=rsem,
            device_id=device,
            device_id_type=MESH,
        )

    RIGHT, LEFT, FAR, PARTNER = (0, 1), (0, 3), (0, 2), (1, 0)
    neighbours = [g.device(*o) for g in groups for o in (RIGHT, LEFT, PARTNER)] + [sibling]

    loads = [
        pltpu.make_async_copy(ref, rows[kind].at[0, pl.ds(0, block), :], load_sem.at[kind])
        for kind, ref in ((0, image_ref), (1, text_ref))
    ]
    for c in loads:
        c.start()
    barrier = pltpu.get_barrier_semaphore()
    for device in neighbours:
        pl.semaphore_signal(barrier, inc=1, device_id=device, device_id_type=MESH)

    row_top[...] = jnp.full(row_top.shape, -1e30, F32)
    row_sum[...] = jnp.zeros(row_sum.shape, F32)
    col_top[...] = jnp.full(col_top.shape, -1e30, F32)
    col_sum[...] = jnp.zeros(col_sum.shape, F32)
    for c in loads:
        c.wait()
    pl.semaphore_wait(barrier, len(neighbours))

    away = sorted(OFFSETS[1:], key=lambda o: -(o[0] + min(o[1], RING - o[1])))
    inner_peers = [groups[0].device(*o) for o in away]
    outer_peers = [groups[1].device(*o, c) for o in away for c in (1, 0)] + [sibling]

    def at(kind, core_step, slot, part=None):
        start, size = PLACE[slot] * block, block
        if part is not None:
            start, size = start + part * half, half
        return rows[kind].at[core_step, pl.ds(start, size), :]

    def copy(kind, src, slot, part, offset):
        n = 2 * (slot - 1) + part
        return remote(
            src,
            at(kind, 0, slot, part),
            gather_send.at[kind],
            gather_recv.at[kind, n],
            groups[kind].device(*offset),
        )

    def gather_copies(kind):
        out = {
            (3, 0): copy(kind, at(kind, 0, 2, 0), 3, 0, RIGHT),
            (3, 1): copy(kind, at(kind, 0, 1, 1), 3, 1, LEFT),
            (6, 0): copy(kind, at(kind, 0, 4, 0), 6, 0, RIGHT),
            (5, 0): copy(kind, at(kind, 0, 4, 0), 5, 0, LEFT),
            (7, 0): copy(kind, at(kind, 0, 6, 0), 7, 0, RIGHT),
            (5, 1): copy(kind, at(kind, 0, 1, 1), 5, 1, PARTNER),
            (6, 1): copy(kind, at(kind, 0, 2, 1), 6, 1, PARTNER),
            (7, 1): copy(kind, at(kind, 0, 3, 1), 7, 1, PARTNER),
        }
        for h in (0, 1):
            mine = at(kind, 0, 0, h)
            for slot, offset in ((2, RIGHT), (1, LEFT), (4, PARTNER)):
                out[slot, h] = copy(kind, mine, slot, h, offset)
        return out

    PARCELS = ((0, 2), (2, 2), (4, 2), (6, 1), (7, 1))

    def fwd(kind, n):
        first, count = PARCELS[n]
        here = pl.ds(first * block, count * block)
        return remote(
            rows[kind].at[0, here, :],
            rows[kind].at[1, here, :],
            fwd_send.at[kind],
            fwd_recv.at[kind, n],
            sibling,
        )

    copies = [gather_copies(kind) for kind in (0, 1)]
    fwds = [[fwd(kind, n) for n in range(len(PARCELS))] for kind in (0, 1)]

    def start(*keys):
        for key in keys:
            for kind in (0, 1):
                copies[kind][key].start()

    def arrived(*keys):
        for key in keys:
            for kind in (0, 1):
                copies[kind][key].wait_recv()

    def forward(*parcels):
        for n in parcels:
            for kind in (1, 0):
                fwds[kind][n].start()

    start((4, 0), (2, 1), (1, 1), (4, 1), (2, 0), (1, 0))

    mine = pl.ds(0, block)
    product = image_rows[0, mine, :].astype(F32) * text_rows[0, mine, :].astype(F32)
    positive = scale * jnp.sum(product, 0, keepdims=True)
    positive = add_up(positive[:, i : i + 128] for i in range(0, width, 128))

    def multiply(a, b, c):
        image = image_rows[0, pl.ds(a * pair, pair), :]
        text = text_rows[c, pl.ds(b * pair, pair), :]
        scores[a, b, :, pl.ds(c * pair, pair)] = (scale * LOG2E) * lax.dot_general(
            image, text, (((1,), (1,)), ((), ())), preferred_element_type=F32
        )

    def count(a, b, c):
        step = 32
        k = pl.ds((2 * b + c) * pair, pair)
        old = col_top[:, k]
        top = old
        for r in range(0, pair, step):
            value = scores[a, b, pl.ds(r, step), pl.ds(c * pair, pair)]
            top = jnp.maximum(top, jnp.max(value.reshape(step // 8, 8, pair), 0))
        total = col_sum[:, k] * jnp.exp2(old - top)
        for r in range(0, pair, step):
            value = scores[a, b, pl.ds(r, step), pl.ds(c * pair, pair)]
            here = pl.ds(a * pair + r, step)
            lanes = [value[:, i : i + 128] for i in range(0, pair, 128)]
            before = row_top[here, :]
            row = functools.reduce(jnp.maximum, lanes, before)
            row_sum[here, :] = row_sum[here, :] * jnp.exp2(before - row) + add_up(
                [jnp.exp2(lane - row) for lane in lanes]
            )
            row_top[here, :] = row
            value = value.reshape(step // 8, 8, pair)
            total = total + jnp.sum(jnp.exp2(value - top[None]), 0)
        col_top[:, k] = top
        col_sum[:, k] = total

    waiting = []

    def tiles(todo):
        for tile in todo:
            multiply(*tile)
            if waiting:
                count(*waiting.pop())
            waiting.append(tile)

    def shell(n, *parcels):
        tiles([(n, b, c) for b in range(n) for c in (0, 1)])
        tiles([(a, n, 0) for a in range(n + 1)])
        sib_arrived(*parcels)
        tiles([(a, n, 1) for a in range(n + 1)])

    def sib_arrived(*parcels):
        for n in parcels:
            fwds[1][n].wait_recv()

    arrived((1, 1))
    start((3, 1), (5, 1))
    arrived((4, 0))
    start((6, 0), (5, 0))
    arrived((2, 1))
    start((6, 1))
    arrived((2, 0))
    start((3, 0))
    arrived((1, 0))
    arrived((4, 1))
    forward(0, 1)
    arrived((3, 1))
    start((7, 1))
    arrived((6, 0))
    start((7, 0))
    shell(0, 0)
    shell(1, 1)
    arrived((3, 0), (5, 0), (5, 1))
    forward(2)
    arrived((6, 1))
    forward(3)
    shell(2, 2)
    for kind in (1, 0):
        for h in (1, 0):
            copies[kind][7, h].wait_recv()
        fwds[kind][4].start()
    shell(3, 3, 4)
    count(*waiting.pop())

    def lse(top, total):
        most = jnp.max(top, 0, keepdims=True)
        total = jnp.sum(total * jnp.exp2(top - most), 0, keepdims=True)
        return most + LOG2E * jnp.log(total)

    for slot, offset in enumerate(OFFSETS):
        place = PLACE[slot]
        for c in (0, 1):
            o = groups[1].index(*offset, c)
            k = pl.ds((place // 2) * 2 * pair + c * pair + (place % 2) * block, block)
            col_stats[outer, pl.ds(o, 1), :] = lse(col_top[:, k], col_sum[:, k])
    for slot, offset in enumerate(OFFSETS):
        i = groups[0].index(*offset)
        r = pl.ds(PLACE[slot] * block, block)
        row_stats[inner, pl.ds(i, 1), :] = lse(
            jnp.transpose(row_top[r, :]), jnp.transpose(row_sum[r, :])
        )
    row_stats[inner, pl.ds(SLOTS, 8), :] = jnp.concatenate(
        [positive, jnp.zeros((7, 128), F32)], 0
    )

    def spread(ref, me, ssem, rsem, peers):
        for device in peers:
            remote(ref.at[me], ref.at[me], ssem, rsem, device).start()
        every = ref.at[pl.ds(0, len(peers))]
        return remote(every, every, ssem, rsem, sibling)

    col_out = spread(col_stats, outer, col_ssem.at[0], col_rsem.at[0], outer_peers)
    row_out = spread(row_stats, inner, row_ssem.at[0], row_rsem.at[0], inner_peers)
    row_out.wait_recv()
    col_out.wait_recv()

    def combine(ref, count):
        values = [ref[n, 0:count, :] for n in range(count)]
        top = functools.reduce(jnp.maximum, values)
        return top + LOG2E * jnp.log(add_up([jnp.exp2(value - top) for value in values]))

    row_value = combine(row_stats, SLOTS)
    col_value = combine(col_stats, 2 * SLOTS)
    row_lse[...] = row_value
    col_lse[...] = col_value
    for slot, offset in enumerate(OFFSETS):
        i = groups[0].index(*offset)
        line = row_lse[pl.ds(i, 1), :]
        place = PLACE[slot]
        row_wide[pl.ds(place * block, block), :] = jnp.transpose(
            jnp.broadcast_to(line, (block, block))
        )
        for c in (0, 1):
            o = groups[1].index(*offset, c)
            k = pl.ds((place // 2) * 2 * pair + c * pair + (place % 2) * block, block)
            col_wide[:, k] = col_lse[pl.ds(o, 1), :]

    def weigh(a, b):
        step = 32
        for r in range(0, pair, step):
            here = pl.ds(a * pair + r, step)
            line = jnp.concatenate([row_wide[here, :]] * 2, 1)
            for c, out in ((0, w_own), (1, w_other)):
                value = scores[a, b, pl.ds(r, step), pl.ds(c * pair, pair)]
                there = pl.ds((2 * b + c) * pair, pair)
                weight = jnp.exp2(value - line) + jnp.exp2(value - col_wide[:, there])
                out[b, here, :] = weight.astype(BF16)

    def w_copy(n, b, r):
        return remote(w_other.at[b, r, :], w_got.at[b, r, :], w_ssem.at[n], w_rsem.at[n], sibling)

    w_copies = [[w_copy(b, b, pl.ds(0, 4 * pair))] for b in range(3)]
    w_copies.append([w_copy(3 + a, 3, pl.ds(a * pair, pair)) for a in range(4)])

    weighed = set()

    def weigh_jobs(g):
        todo = [t for t in [(a, g) for a in range(4)] + [(g, b) for b in range(4)] if t not in weighed]
        todo = sorted(set(todo), key=todo.index)
        weighed.update(todo)
        return [functools.partial(weigh, *t) for t in todo]

    paired = add_up([row_stats[n, pl.ds(SLOTS, 8), :] for n in range(SLOTS)])
    shares = (
        row_value * (1.0 / LOG2E) - 2.0 * paired,
        (col_value[0:8] + col_value[8:16]) * (1.0 / LOG2E),
    )
    high, low, core = groups[0].highs[0], groups[0].lows[0], groups[0].cores[0]
    who = (2 * lax.rem(high + low, 2) + core, high)
    others = (
        [groups[1].device(1, 0, 1), groups[1].device(*PARTNER), sibling],
        [groups[0].device(*PARTNER)],
    )
    losses = ((image_loss, image_loss_ring), (text_loss, text_loss_ring))

    def loss_near(kind):
        losses[kind][0][who[kind]] = shares[kind]
        return spread(
            losses[kind][0], who[kind], loss_ssem.at[kind, 0], loss_rsem.at[kind, 0], others[kind]
        )

    def loss_ring(kind, near):
        group = groups[1 - kind]
        near.wait_recv()
        ref = losses[kind][0]
        losses[kind][1][group.place] = add_up([ref[n] for n in range(ref.shape[0])])
        return spread(
            losses[kind][1],
            group.place,
            loss_ssem.at[kind, 1],
            loss_rsem.at[kind, 1],
            [group.device(0, n) for n in (2, 1, 3)],
        )

    def loss_sum(kind, ring):
        ring.wait_recv()
        return add_up([losses[kind][1][n] for n in range(RING)])

    parts = (image_part, text_part)
    sends = (image_send, text_send)
    gots = (image_got, text_got)

    def lines(slot, h):
        return pl.ds(PLACE[slot] * block + h * half, half)

    def red_copies(kind):
        way = {(7, 0): RIGHT, (5, 0): RIGHT, (6, 0): LEFT, (3, 0): RIGHT, (3, 1): LEFT}
        way.update({(1, h): RIGHT for h in (0, 1)})
        way.update({(2, h): LEFT for h in (0, 1)})
        way.update({(slot, 1): PARTNER for slot in (4, 5, 6, 7)})
        way[4, 0] = PARTNER
        return {
            key: remote(
                sends[kind].at[lines(*key), :],
                gots[kind].at[n],
                red_ssem.at[kind],
                red_rsem.at[kind, n],
                groups[kind].device(*way[key]),
            )
            for n, key in enumerate(sorted(way))
        }

    reds = [red_copies(kind) for kind in (0, 1)]
    numbers = {key: n for n, key in enumerate(sorted(reds[0]))}

    def total_of(kind, slot, h, *keys):
        value = parts[kind][lines(slot, h), :]
        for key in keys:
            reds[kind][key].wait_recv()
            value = value + gots[kind][numbers[key]].astype(F32)
        return value

    READY = {(7, 0), (7, 1), (6, 0), (6, 1), (3, 0), (5, 1), (2, 0), (4, 1)}

    def pass_on(kind, slot, h, *keys):
        if (slot, h) not in READY:
            sends[kind][lines(slot, h), :] = total_of(kind, slot, h, *keys).astype(BF16)
        reds[kind][slot, h].start()

    def product(kind, g, jobs=()):
        chunks = width // pair
        for n in range(chunks):
            k = pl.ds(n * pair, pair)
            if kind == 0:
                value = add_up(
                    [
                        jnp.dot(
                            jnp.concatenate([w[b, pl.ds(g * pair, pair), :] for b in range(4)], 1),
                            text_rows[c, :, k],
                            preferred_element_type=F32,
                        )
                        for c, w in ((0, w_own), (1, w_other))
                    ]
                )
            else:
                value = add_up(
                    [
                        lax.dot_general(
                            w[g],
                            image_rows[c, :, k],
                            (((0,), (0,)), ((), ())),
                            preferred_element_type=F32,
                        )
                        for c, w in ((0, w_own), (1, w_got))
                    ]
                )
            for job in jobs[n::chunks]:
                job()
            for i in range(4):
                slot, h = PLACE.index(2 * g + i // 2), i % 2
                piece = value[i * half : (i + 1) * half]
                if (slot, h) in READY:
                    sends[kind][lines(slot, h), k] = piece.astype(BF16)
                else:
                    parts[kind][lines(slot, h), k] = piece

    def image(g, beside=None):
        product(0, g, weigh_jobs(beside) if beside is not None else ())
        if beside is not None:
            for c in w_copies[beside]:
                c.start()

    def text(g, beside=None):
        for c in w_copies[g]:
            c.wait_recv()
        product(1, g, weigh_jobs(beside) if beside is not None else ())
        if beside is not None:
            for c in w_copies[beside]:
                c.start()

    for n, job in enumerate(weigh_jobs(3)):
        job()
        if n < 4:
            w_copies[3][n].start()
    product(0, 3, weigh_jobs(2))
    pass_on(0, 7, 1)
    pass_on(0, 7, 0)
    w_copies[2][0].start()
    near_copies = [loss_near(kind) for kind in (0, 1)]
    pass_on(0, 6, 1)
    for c in fwds[0]:
        c.wait_recv()
    text(3, 1)
    pass_on(1, 7, 1)
    pass_on(1, 7, 0)
    pass_on(0, 6, 0)
    image(2, 0)
    pass_on(1, 6, 1)
    pass_on(0, 3, 0)
    ring_copies = [loss_ring(0, near_copies[0])]
    text(2)
    pass_on(1, 3, 0)
    pass_on(1, 5, 1)
    pass_on(1, 6, 0)
    pass_on(0, 5, 1)
    ring_copies.append(loss_ring(1, near_copies[1]))
    image(1)
    pass_on(0, 3, 1, (7, 1))
    pass_on(0, 5, 0, (7, 0))
    text(1)
    pass_on(1, 5, 0, (7, 0))
    pass_on(1, 3, 1, (7, 1))
    image(0)
    pass_on(0, 4, 1)
    pass_on(0, 2, 0)
    pass_on(0, 1, 0, (3, 0))
    text(0)
    pass_on(1, 4, 1)
    pass_on(1, 2, 0)
    pass_on(1, 1, 0, (3, 0))
    pass_on(0, 2, 1, (6, 1), (3, 1))
    pass_on(1, 1, 1, (5, 1))
    pass_on(0, 4, 0, (5, 0), (6, 0))
    pass_on(0, 1, 1, (5, 1))
    pass_on(1, 4, 0, (5, 0), (6, 0))
    pass_on(1, 2, 1, (6, 1), (3, 1))
    loss = loss_sum(0, ring_copies[0]) + loss_sum(1, ring_copies[1])
    loss = jnp.sum(jnp.sum(loss, 0, keepdims=True), 1, keepdims=True)
    total_rows = block * 2 * SLOTS * SLOTS
    loss_ref[...] = jnp.broadcast_to(loss / (2.0 * total_rows), loss_ref.shape)

    for h, keys in ((0, ((1, 0), (2, 0), (4, 0))), (1, ((4, 1), (1, 1), (2, 1)))):
        r = pl.ds(h * half, half)
        for kind, out in ((0, image_out), (1, text_out)):
            out[r, :] = total_of(kind, 0, h, *keys)

    for kind in (0, 1):
        sent = rows[kind].at[0, pl.ds(0, 14 * half), :]
        remote(sent, sent, gather_send.at[kind], gather_recv.at[kind, 0], sibling).wait_send()
        sent = rows[kind].at[0]
        remote(sent, sent, fwd_send.at[kind], fwd_recv.at[kind, 0], sibling).wait_send()
        sent = sends[kind].at[pl.ds(0, 14 * half), :]
        remote(sent, sent, red_ssem.at[kind], red_rsem.at[kind, 0], sibling).wait_send()
    for c in sum(w_copies, []) + near_copies + ring_copies + [row_out, col_out]:
        c.wait_send()


def finish(image_ref, text_ref, loss_ref, image_sum, text_sum, loss_out, image_out, text_out):
    half_scale = 0.5 * image_ref.shape[1] ** (-0.5)
    image_out[...] = half_scale * (image_sum[...] - 2.0 * text_ref[...].astype(F32))
    text_out[...] = half_scale * (text_sum[...] - 2.0 * image_ref[...].astype(F32))
    loss_out[0, 0] = loss_ref[0, 0]


def on_device(image_embed, text_embed):
    block, width = image_embed.shape
    group = SLOTS * block
    dma = pltpu.SemaphoreType.DMA
    shape = jax.ShapeDtypeStruct
    vmem = pl.BlockSpec(memory_space=pltpu.VMEM)
    loss, image_sum, text_sum = pl.pallas_call(
        kernel,
        out_shape=(
            shape((8, 128), F32),
            shape((block, width), F32),
            shape((block, width), F32),
        ),
        in_specs=[pl.BlockSpec(memory_space=pltpu.HBM)] * 2,
        out_specs=(vmem, vmem, vmem),
        scratch_shapes=[
            pltpu.VMEM((2, group, width), BF16),
            pltpu.VMEM((2, group, width), BF16),
            pltpu.VMEM((4, 4, 2 * block, 4 * block), F32),
            pltpu.VMEM((group, 128), F32),
            pltpu.VMEM((group, 128), F32),
            pltpu.VMEM((8, 2 * group), F32),
            pltpu.VMEM((8, 2 * group), F32),
            pltpu.VMEM((SLOTS, 2 * SLOTS, 128), F32),
            pltpu.VMEM((2 * SLOTS, 2 * SLOTS, 128), F32),
            pltpu.VMEM((SLOTS, 128), F32),
            pltpu.VMEM((2 * SLOTS, 128), F32),
            pltpu.VMEM((group, 128), F32),
            pltpu.VMEM((1, 2 * group), F32),
            pltpu.VMEM((4, group, 2 * block), BF16),
            pltpu.VMEM((4, group, 2 * block), BF16),
            pltpu.VMEM((4, group, 2 * block), BF16),
            pltpu.VMEM((group, width), F32),
            pltpu.VMEM((group, width), F32),
            pltpu.VMEM((group, width), BF16),
            pltpu.VMEM((group, width), BF16),
            pltpu.VMEM((14, block // 2, width), BF16),
            pltpu.VMEM((14, block // 2, width), BF16),
            pltpu.VMEM((4, 8, 128), F32),
            pltpu.VMEM((RING, 8, 128), F32),
            pltpu.VMEM((2, 8, 128), F32),
            pltpu.VMEM((RING, 8, 128), F32),
            dma((2,)),
            dma((2, 14)),
            dma((2,)),
            dma((2, 5)),
            dma((1,)),
            dma((1,)),
            dma((1,)),
            dma((1,)),
            dma((2, 2)),
            dma((2, 2)),
            dma((7,)),
            dma((7,)),
            dma((2,)),
            dma((2, 14)),
            dma((2,)),
        ],
        compiler_params=pltpu.CompilerParams(
            collective_id=0, has_side_effects=True, vmem_limit_bytes=56 * 2**20
        ),
    )(image_embed, text_embed)
    loss, image_grad, text_grad = pl.pallas_call(
        finish,
        out_shape=(
            shape((1, 1), F32),
            shape((block, width), F32),
            shape((block, width), F32),
        ),
        in_specs=[vmem] * 5,
        out_specs=(pl.BlockSpec(memory_space=pltpu.SMEM), vmem, vmem),
    )(image_embed, text_embed, loss, image_sum, text_sum)
    return loss.reshape(()), image_grad, text_grad


def solution(mesh):
    return jax.shard_map(
        on_device,
        mesh=mesh,
        in_specs=(P(("inner", "outer"), None), P(("inner", "outer"), None)),
        out_specs=(P(), P(("inner", "outer"), None), P(("inner", "outer"), None)),
        check_vma=False,
    )
```

profile of v0, /device:TPU:1, one launch (start us, length us, event | category | flops | bytes accessed | tf_op | source)
XLA Modules:
  0.0 51.5 jit_solution(10670453837888175094)
XLA Ops:
  0.6 48.4 %shard_map.49 = (f32[8,128]{1,0:T(8,128)}, f32[128,768]{1,0:T(8,128)}, f32[128,768]{1,0:T(8,128)}) custom-call(bf16[128,768]{1,0:T(8,128)(2,1)} %image_ref.3, bf16[128,768]{1,0:T(8,128)(2,1)} %text_ref.3), custom_call_target="tpu_custom_call" | custom-call | tf_op jit(solution)/shard_map/pallas_call | solution.py:577
  49.0 2.3 %shard_map.50 = (f32[1,1]{1,0:T(1,128)}, f32[128,768]{1,0:T(8,128)}, f32[128,768]{1,0:T(8,128)}) custom-call(bf16[128,768]{1,0:T(8,128)(2,1)} %image_ref.3, bf16[128,768]{1,0:T(8,128)(2,1)} %text_ref.3, f32[8,128]{1,0:T(8,128)} %get-tuple-element.9.loss_ref, f32[128,768]{1,0:T(8,128)} %get-tuple-element.10.image_sum, f32[128,768]{1,0:T(8,128)} %get-tuple-element.11.text_sum), custom_call_target="tpu_custom_call" | custom-call | tf_op jit(solution)/shard_map/pallas_call | solution.py:633
where the time goes:
time: 52.2 us; the launch traced here: 51.5 us
  Pallas kernels  50.7 us (97%)
  between operations  0.8 us (2%)
    pallas_call x1, Pallas kernels, on_device(): pl.pallas_call(kernel, out_shape=(shape((8, 128), F32), shape((block, wid...  48.4 us
    pallas_call x1, Pallas kernels, on_device(): pl.pallas_call(finish, out_shape=(shape((1, 1), F32), shape((block, width...  2.25 us

commit v1 on v0

--- a/solution.py
+++ b/solution.py
@@ -503,42 +503,42 @@
     pass_on(0, 7, 0)
     w_copies[2][0].start()
     near_copies = [loss_near(kind) for kind in (0, 1)]
+    pass_on(0, 6, 0)
     pass_on(0, 6, 1)
     for c in fwds[0]:
         c.wait_recv()
     text(3, 1)
     pass_on(1, 7, 1)
     pass_on(1, 7, 0)
-    pass_on(0, 6, 0)
     image(2, 0)
-    pass_on(1, 6, 1)
     pass_on(0, 3, 0)
+    pass_on(1, 6, 0)
+    text(2)
     ring_copies = [loss_ring(0, near_copies[0])]
-    text(2)
+    pass_on(0, 5, 1)
     pass_on(1, 3, 0)
     pass_on(1, 5, 1)
-    pass_on(1, 6, 0)
-    pass_on(0, 5, 1)
+    text(1)
     ring_copies.append(loss_ring(1, near_copies[1]))
+    pass_on(0, 5, 0, (7, 0))
+    pass_on(1, 6, 1)
     image(1)
+    pass_on(1, 5, 0, (7, 0))
     pass_on(0, 3, 1, (7, 1))
-    pass_on(0, 5, 0, (7, 0))
-    text(1)
-    pass_on(1, 5, 0, (7, 0))
     pass_on(1, 3, 1, (7, 1))
     image(0)
     pass_on(0, 4, 1)
     pass_on(0, 2, 0)
-    pass_on(0, 1, 0, (3, 0))
     text(0)
     pass_on(1, 4, 1)
+    pass_on(0, 1, 0, (3, 0))
+    pass_on(1, 1, 0, (3, 0))
     pass_on(1, 2, 0)
-    pass_on(1, 1, 0, (3, 0))
-    pass_on(0, 2, 1, (6, 1), (3, 1))
+    pass_on(0, 4, 0, (5, 0), (6, 0))
     pass_on(1, 1, 1, (5, 1))
-    pass_on(0, 4, 0, (5, 0), (6, 0))
     pass_on(0, 1, 1, (5, 1))
     pass_on(1, 4, 0, (5, 0), (6, 0))
+    pass_on(0, 2, 1, (6, 1), (3, 1))
     pass_on(1, 2, 1, (6, 1), (3, 1))
     loss = loss_sum(0, ring_copies[0]) + loss_sum(1, ring_copies[1])
     loss = jnp.sum(jnp.sum(loss, 0, keepdims=True), 1, keepdims=True)

time: 52.2 us -> 51.7 us (level); the launches traced: 51.5 us -> 51.6 us
  no operation moved by 1% of the time
where the time goes in v1:
time: 51.7 us; the launch traced here: 51.6 us
  Pallas kernels  50.8 us (98%)
  between operations  0.8 us (2%)
    pallas_call x1, Pallas kernels, on_device(): pl.pallas_call(kernel, out_shape=(shape((8, 128), F32), shape((block, wid...  48.5 us
    pallas_call x1, Pallas kernels, on_device(): pl.pallas_call(finish, out_shape=(shape((1, 1), F32), shape((block, width...  2.25 us

profile of v1, /device:TPU:1, one launch (start us, length us, event | category | flops | bytes accessed | tf_op | source)
XLA Modules:
  0.0 51.6 jit_solution(690863502771822836)
XLA Ops:
  0.6 48.5 %shard_map.49 = (f32[8,128]{1,0:T(8,128)}, f32[128,768]{1,0:T(8,128)}, f32[128,768]{1,0:T(8,128)}) custom-call(bf16[128,768]{1,0:T(8,128)(2,1)} %image_ref.3, bf16[128,768]{1,0:T(8,128)(2,1)} %text_ref.3), custom_call_target="tpu_custom_call" | custom-call | tf_op jit(solution)/shard_map/pallas_call | solution.py:577
  49.2 2.3 %shard_map.50 = (f32[1,1]{1,0:T(1,128)}, f32[128,768]{1,0:T(8,128)}, f32[128,768]{1,0:T(8,128)}) custom-call(bf16[128,768]{1,0:T(8,128)(2,1)} %image_ref.3, bf16[128,768]{1,0:T(8,128)(2,1)} %text_ref.3, f32[8,128]{1,0:T(8,128)} %get-tuple-element.9.loss_ref, f32[128,768]{1,0:T(8,128)} %get-tuple-element.10.image_sum, f32[128,768]{1,0:T(8,128)} %get-tuple-element.11.text_sum), custom_call_target="tpu_custom_call" | custom-call | tf_op jit(solution)/shard_map/pallas_call | solution.py:633
